TPU v7x, 256 devices: a whole 4x4x8 slice. The times are simulated.
256 devices in a mesh: dp: 8 (over y, z_lo), seq: 32 (over x, z_hi, core).
Axes of the slice: x: 4, y: 4, z: 8 (z_hi: 4, z_lo: 2; z = z_hi * 2 + z_lo), core: 2. Of those that a mesh axis runs over, the one named last changes fastest.
Arguments:
- queries: bfloat16 [32768, 1024], P(('dp', 'seq')), parts along dimension 0, may hold values from -8 to 8
- key_rows: bfloat16 [32768, 1024], P(('dp', 'seq')), parts along dimension 0, may hold values from -8 to 8
- value_rows: bfloat16 [32768, 1024], P(('dp', 'seq')), parts along dimension 0, may hold values from -6 to 6
- out_cotangent: bfloat16 [32768, 1024], P(('dp', 'seq')), parts along dimension 0, may hold values from -6 to 6
- scale_starts: int32 [96], P('dp'), parts along dimension 0, may hold values from 0 to 1031, as said below
Outputs:
- attended: bfloat16 [32768, 1024], P(('dp', 'seq')), parts along dimension 0
- query_grad: bfloat16 [32768, 1024], P(('dp', 'seq')), parts along dimension 0
- key_grad: bfloat16 [32768, 1024], P(('dp', 'seq')), parts along dimension 0
- value_grad: bfloat16 [32768, 1024], P(('dp', 'seq')), parts along dimension 0
There are 8 independent parts, one for each index of `dp`. A program takes and returns all parts, laid end to end along the dimension named above; each array names one. Nothing has to cross between parts.
Inputs may be any that keep to these rules, and one draw needn't show every extreme that they name: `scale_starts`: the first token of each of the 12 scales in order: the first is 0, each is larger than the one before, all lie below 4096.
All inputs are finite; a program needn't handle non-finite values.
Results may differ from a plain program's by a relative error of at most 0.011.
Values may be sent and summed in bfloat16 or wider, within the bound.
A program may use at most 128 MiB of HBM per device.

v0:
```python
import math

import jax
import jax.numpy as jnp
from jax import lax
from jax.sharding import PartitionSpec as P

HEADS = 8
HEAD_DIM = 128


NEG_LARGE = -1e30
block_limit = 512


def scale_index(positions, scale_starts):
    reached = (positions[:, None] >= scale_starts[None, :]).astype(jnp.int32)
    return jnp.sum(reached, axis=1) - 1


def per_device(queries, key_rows, value_rows, out_cotangent, scale_starts):
    shard_rows = queries.shape[0]
    factor = 1.0 / math.sqrt(HEAD_DIM)
    local_index = lax.axis_index("seq") * shard_rows + jnp.arange(shard_rows, dtype=jnp.int32)
    local_scale = scale_index(local_index, scale_starts)
    query_heads = queries.reshape(shard_rows, HEADS, HEAD_DIM)
    cotangent_heads = out_cotangent.reshape(shard_rows, HEADS, HEAD_DIM)
    key_heads = key_rows.reshape(shard_rows, HEADS, HEAD_DIM)
    value_heads = value_rows.reshape(shard_rows, HEADS, HEAD_DIM)

    def guarded(update, carried, operands, visible):
        return update(carried, *operands, visible)

    def key_visibility(indices):
        block_scale = scale_index(indices, scale_starts)
        return block_scale[None, :] <= local_scale[:, None]

    def stats_update(carried, block_keys, visible):
        running_max, running_sum = carried
        scores = (
            jnp.einsum("qhd,khd->hqk", query_heads, block_keys, preferred_element_type=jnp.float32)
            * factor
        )
        masked = jnp.where(visible[None], scores, NEG_LARGE)
        new_max = jnp.maximum(running_max, jnp.max(masked, axis=2))
        terms = jnp.where(visible[None], jnp.exp(masked - new_max[:, :, None]), 0.0)
        new_sum = jnp.exp(running_max - new_max) * running_sum + jnp.sum(terms, axis=2)
        return (new_max, new_sum)

    stats_init = (
        jnp.full((HEADS, shard_rows), NEG_LARGE, jnp.float32),
        jnp.zeros((HEADS, shard_rows), jnp.float32),
    )
    carried = stats_init
    piece_keys = lax.all_gather(key_rows, "seq", axis=0, tiled=True)
    first_row = jnp.int32(0)
    piece_rows = piece_keys.shape[0]
    for offset in range(0, piece_rows, block_limit):
        block_size = min(block_limit, piece_rows - offset)
        indices = first_row + offset + jnp.arange(block_size, dtype=jnp.int32)
        block_keys = piece_keys[offset : offset + block_size].reshape(block_size, HEADS, HEAD_DIM)
        carried = guarded(stats_update, carried, (block_keys,), key_visibility(indices))
    running_max, running_sum = carried
    log_norm = running_max + jnp.log(running_sum)

    def forward_update(carried, block_keys, block_values, visible):
        value_total, mixed_total, key_total, inner_total = carried
        scores = (
            jnp.einsum("qhd,khd->hqk", query_heads, block_keys, preferred_element_type=jnp.float32)
            * factor
        )
        weights = jnp.exp(jnp.where(visible[None], scores - log_norm[:, :, None], NEG_LARGE))
        prob_half = weights.astype(jnp.bfloat16)
        prob_grad = jnp.einsum(
            "qhd,khd->hqk", cotangent_heads, block_values, preferred_element_type=jnp.float32
        )
        product = weights * prob_grad
        inner_total = inner_total + jnp.sum(product, axis=2)
        mixed_half = product.astype(jnp.bfloat16)
        value_total = value_total + jnp.einsum(
            "hqk,khd->hqd", prob_half, block_values, preferred_element_type=jnp.float32
        )
        mixed_total = mixed_total + jnp.einsum(
            "hqk,khd->hqd", mixed_half, block_keys, preferred_element_type=jnp.float32
        )
        key_total = key_total + jnp.einsum(
            "hqk,khd->hqd", prob_half, block_keys, preferred_element_type=jnp.float32
        )
        return (value_total, mixed_total, key_total, inner_total)

    state_zeros = jnp.zeros((HEADS, shard_rows, HEAD_DIM), jnp.float32)
    initial = (state_zeros, state_zeros, state_zeros, jnp.zeros((HEADS, shard_rows), jnp.float32))
    carried = initial
    first_row = jnp.int32(0)
    piece_keys = lax.all_gather(key_rows, "seq", axis=0, tiled=True)
    piece_values = lax.all_gather(value_rows, "seq", axis=0, tiled=True)
    piece_rows = piece_keys.shape[0]
    for offset in range(0, piece_rows, block_limit):
        block_size = min(block_limit, piece_rows - offset)
        indices = first_row + offset + jnp.arange(block_size, dtype=jnp.int32)
        block_keys = piece_keys[offset : offset + block_size].reshape(block_size, HEADS, HEAD_DIM)
        block_values = piece_values[offset : offset + block_size].reshape(
            block_size, HEADS, HEAD_DIM
        )
        carried = guarded(
            forward_update, carried, (block_keys, block_values), key_visibility(indices)
        )
    value_total, mixed_total, key_total, inner_sum = carried
    attended = (
        jnp.transpose(value_total, (1, 0, 2))
        .reshape(shard_rows, HEADS * HEAD_DIM)
        .astype(jnp.bfloat16)
    )
    query_total = (mixed_total - inner_sum[:, :, None] * key_total) * factor
    query_grad = (
        jnp.transpose(query_total, (1, 0, 2))
        .reshape(shard_rows, HEADS * HEAD_DIM)
        .astype(jnp.bfloat16)
    )
    norm_rows, inner_rows = (
        lax.all_gather(log_norm, "seq", axis=1, tiled=True),
        lax.all_gather(inner_sum, "seq", axis=1, tiled=True),
    )

    def backward_update(carried, block_queries, block_cotangent, block_norms, block_inner, visible):
        key_total, value_total = carried
        scores = (
            jnp.einsum("qhd,khd->hqk", block_queries, key_heads, preferred_element_type=jnp.float32)
            * factor
        )
        weights = jnp.exp(jnp.where(visible[None], scores - block_norms[:, :, None], NEG_LARGE))
        prob_grad = jnp.einsum(
            "qhd,khd->hqk", block_cotangent, value_heads, preferred_element_type=jnp.float32
        )
        score_grad = weights * (prob_grad - block_inner[:, :, None])
        value_total = value_total + jnp.einsum(
            "hqk,qhd->khd",
            weights.astype(jnp.bfloat16),
            block_cotangent,
            preferred_element_type=jnp.float32,
        )
        key_total = key_total + jnp.einsum(
            "hqk,qhd->khd",
            score_grad.astype(jnp.bfloat16),
            block_queries,
            preferred_element_type=jnp.float32,
        )
        return (key_total, value_total)

    grad_zeros = jnp.zeros((shard_rows, HEADS, HEAD_DIM), jnp.float32)
    carried = (grad_zeros, grad_zeros)
    first_row = jnp.int32(0)
    piece_queries = lax.all_gather(queries, "seq", axis=0, tiled=True)
    piece_cotangent = lax.all_gather(out_cotangent, "seq", axis=0, tiled=True)
    piece_rows = piece_queries.shape[0]
    for offset in range(0, piece_rows, block_limit):
        block_size = min(block_limit, piece_rows - offset)
        indices = first_row + offset + jnp.arange(block_size, dtype=jnp.int32)
        block_scale = scale_index(indices, scale_starts)
        visible = local_scale[None, :] <= block_scale[:, None]
        block_queries = piece_queries[offset : offset + block_size].reshape(
            block_size, HEADS, HEAD_DIM
        )
        block_cotangent = piece_cotangent[offset : offset + block_size].reshape(
            block_size, HEADS, HEAD_DIM
        )
        block_norms = lax.dynamic_slice_in_dim(norm_rows, offset, block_size, axis=1)
        block_inner = lax.dynamic_slice_in_dim(inner_rows, offset, block_size, axis=1)
        carried = guarded(
            backward_update,
            carried,
            (block_queries, block_cotangent, block_norms, block_inner),
            visible,
        )
    key_total, value_total = carried
    key_grad = (key_total * factor).reshape(shard_rows, HEADS * HEAD_DIM).astype(jnp.bfloat16)
    value_grad = value_total.reshape(shard_rows, HEADS * HEAD_DIM).astype(jnp.bfloat16)
    return (attended, query_grad, key_grad, value_grad)


def solution(mesh):
    placed = (
        P(("dp", "seq"), None),
        P(("dp", "seq"), None),
        P(("dp", "seq"), None),
        P(("dp", "seq"), None),
        P("dp"),
    )
    return jax.shard_map(
        per_device,
        mesh=mesh,
        in_specs=placed,
        out_specs=(
            P(("dp", "seq"), None),
            P(("dp", "seq"), None),
            P(("dp", "seq"), None),
            P(("dp", "seq"), None),
        ),
        check_vma=False,
    )
```

profile of v0, /device:TPU:1, one launch (start us, length us, event | category | flops | bytes accessed | tf_op | source)
XLA Modules:
  0.0 441.0 jit_solution(8905427170785828357)
XLA Ops:
  16.4 84.6 %all-gather.5.cloned.1.call-done = bf16[4096,1024]{0,1:T(8,128)(2,1)} async-done(((bf16[128,1024]{0,1:T(8,128)(2,1)}), bf16[4096,1024]{0,1:T(8,128)(2,1)}) %all-gather.5.cloned.1.call-update) | async-done | bytes 8388624 | tf_op jit(solution)/shard_map/all_gather | solution.py:95
  100.9 5.4 %fusion.171 = (bf16[512,1024]{0,1:T(8,128)(2,1)}, bf16[512,1024]{0,1:T(8,128)(2,1)S(1)}, bf16[512,1024]{0,1:T(8,128)(2,1)S(1)}, bf16[512,1024]{0,1:T(8,128)(2,1)...) fusion(bf16[4096,1024]{0,1:T(8,128)(2,1)} %all-gather.5.cloned., ...), kind=kLoop, calls=%fused_computation.260 | loop fusion | bytes 16777216 | tf_op jit(solution)/shard_map/slice | solution.py:61
  111.0 66.8 %all-gather.7.cloned.1.call-done = bf16[4096,1024]{1,0:T(8,128)(2,1)} async-done(((bf16[128,1024]{1,0:T(8,128)(2,1)}), bf16[4096,1024]{1,0:T(8,128)(2,1)}) %all-gather.7.cloned.1.call-update) | async-done | bytes 8388624 | tf_op jit(solution)/shard_map/all_gather | solution.py:96
  177.8 6.1 %fusion.170 = (bf16[512,1024]{1,0:T(8,128)(2,1)}, bf16[512,1024]{1,0:T(8,128)(2,1)}, bf16[512,1024]{1,0:T(8,128)(2,1)}, bf16[512,1024]{1,0:T(8,128)(2,1)}, bf16[...) fusion(bf16[4096,1024]{1,0:T(8,128)(2,1)} %all-gather.7.cloned.1.ca, ...), kind=kLoop, calls=%fused_computation.259 | loop fusion | bytes 16777216 | tf_op jit(solution)/shard_map/slice | solution.py:102
  185.7 2.3 copy.250
  188.0 2.3 copy.251
  190.3 2.3 copy.252
  192.6 2.3 copy.253
  194.9 2.3 copy.254
  197.2 2.3 copy.255
  199.5 2.3 copy.256
  201.8 2.4 copy.257
  230.1 3.0 fusion.174
  259.0 47.2 %all_gather.22 = f32[8,4096]{1,0:T(8,128)S(1)} all-gather(f32[8,128]{1,0:T(8,128)S(1)} %log_add_fusion), channel_id=1, replica_groups=mesh['dp'=8,'seq'=32] {'seq'}, dimensions={1}, use_global_device_ids=true | all-gather | bytes 135168 | tf_op jit(solution)/shard_map/all_gather | solution.py:121
  306.2 47.9 %all_gather.24 = f32[8,4096]{1,0:T(8,128)S(1)} all-gather(f32[8,128]{1,0:T(8,128)S(1)} %add_add_fusion), channel_id=1, replica_groups=mesh['dp'=8,'seq'=32] {'seq'}, dimensions={1}, use_global_device_ids=true | all-gather | bytes 135168 | tf_op jit(solution)/shard_map/all_gather | solution.py:122
  354.8 6.1 %fusion.169 = (bf16[512,1024]{0,1:T(8,128)(2,1)}, bf16[512,1024]{0,1:T(8,128)(2,1)}, bf16[512,1024]{0,1:T(8,128)(2,1)}, bf16[512,1024]{0,1:T(8,128)(2,1)}, bf16[...) fusion(bf16[4096,1024]{0,1:T(8,128)(2,1)} %all-gather.9.cloned., ...), kind=kLoop, calls=%fused_computation.258 | loop fusion | bytes 16777216 | tf_op jit(solution)/shard_map/slice | solution.py:161
  363.9 6.0 %fusion.168 = (bf16[512,1024]{0,1:T(8,128)(2,1)S(1)}, bf16[512,1024]{0,1:T(8,128)(2,1)S(1)}, bf16[512,1024]{0,1:T(8,128)(2,1)}, bf16[512,1024]{0,1:T(8,128)(2,1)...) fusion(bf16[4096,1024]{0,1:T(8,128)(2,1)} %all-gather.11.cloned, ...), kind=kLoop, calls=%fused_computation.257 | loop fusion | bytes 16777216 | tf_op jit(solution)/shard_map/slice | solution.py:164
  371.2 3.8 fusion.8
  375.0 3.7 select_exponential_fusion.6
  380.8 2.1 select_exponential_fusion.4
  382.9 2.2 select_exponential_fusion.3
  385.1 2.1 select_exponential_fusion.2
  387.2 2.1 select_exponential_fusion.1
  389.3 2.2 select_exponential_fusion
  391.5 3.9 fusion.28
  395.4 4.3 fusion.27
  399.7 3.9 fusion.26
  403.6 4.3 fusion.25
  407.9 3.9 fusion.24
  411.8 3.9 fusion.23
  415.7 3.8 fusion.30
  421.3 2.6 convolution_add_fusion.6
  (277 shorter events, 86.0 us)
Async XLA Ops:
  7.2 6.5 %copy-start.90 = (s32[12]{0:T(128)S(1)}, s32[12]{0:T(128)}, u32[]{:S(2)}) copy-start(s32[12]{0:T(128)} %param.9) | copy-start | bytes 148
  7.2 93.8 %all-gather.5.cloned.1.call-start = ((), (), s32[]{:S(2)}) async-start(), calls=%async_computation | async-start | bytes 8650752 | tf_op jit(solution)/shard_map/all_gather | solution.py:95
  9.0 168.7 %all-gather.7.cloned.1.call-start = ((), (), s32[]{:S(2)}) async-start(), calls=%async_computation.1 | async-start | bytes 8650752 | tf_op jit(solution)/shard_map/all_gather | solution.py:96
  9.8 345.0 %all-gather.9.cloned.1.call-start = ((), (), s32[]{:S(2)}) async-start(), calls=%async_computation.2 | async-start | bytes 8650752 | tf_op jit(solution)/shard_map/all_gather | solution.py:153
  11.7 352.3 %all-gather.11.cloned.1.call-start = ((), (), s32[]{:S(2)}) async-start(), calls=%async_computation.3 | async-start | bytes 8650752 | tf_op jit(solution)/shard_map/all_gather | solution.py:154
  16.4 91.0 %copy-start = (bf16[128,1024]{1,0:T(8,128)(2,1)S(1)}, bf16[128,1024]{1,0:T(8,128)(2,1)}, u32[]{:S(2)}) copy-start(bf16[128,1024]{1,0:T(8,128)(2,1)} %param.5) | copy-start | bytes 786436
  100.9 6.4 %copy-start.72 = (pred[128,512]{1,0:T(8,128)(4,1)S(1)}, pred[128,512]{1,0:T(8,128)(4,1)}, u32[]{:S(2)}) copy-start(pred[128,512]{1,0:T(8,128)(4,1)} %get-tuple-element.92) | copy-start | bytes 196612
  106.3 2.8 copy-start.8
  205.6 18.2 %copy-start.25 = (f32[8,128,512]{2,1,0:T(8,128)}, f32[8,128,512]{2,1,0:T(8,128)S(1)}, u32[]{:S(2)}) copy-start(f32[8,128,512]{2,1,0:T(8,128)S(1)} %get-tuple-element.105) | copy-start | bytes 6291460
  206.2 16.4 %copy-start.27 = (f32[8,128,512]{2,1,0:T(8,128)}, f32[8,128,512]{2,1,0:T(8,128)S(1)}, u32[]{:S(2)}) copy-start(f32[8,128,512]{2,1,0:T(8,128)S(1)} %get-tuple-element.107) | copy-start | bytes 6291460
  206.2 2.5 copy-start.4
  206.3 2.5 copy-start.68
  208.2 13.2 %copy-start.29 = (f32[8,128,512]{2,1,0:T(8,128)}, f32[8,128,512]{2,1,0:T(8,128)S(1)}, u32[]{:S(2)}) copy-start(f32[8,128,512]{2,1,0:T(8,128)S(1)} %get-tuple-element.109) | copy-start | bytes 6291460
  209.3 10.9 %copy-start.31 = (f32[8,128,512]{2,1,0:T(8,128)}, f32[8,128,512]{2,1,0:T(8,128)S(1)}, u32[]{:S(2)}) copy-start(f32[8,128,512]{2,1,0:T(8,128)S(1)} %get-tuple-element.111) | copy-start | bytes 6291460
  209.3 2.4 copy-start.19
  210.3 2.8 copy-start.21
  210.8 8.2 %copy-start.33 = (f32[8,128,512]{2,1,0:T(8,128)}, f32[8,128,512]{2,1,0:T(8,128)S(1)}, u32[]{:S(2)}) copy-start(f32[8,128,512]{2,1,0:T(8,128)S(1)} %get-tuple-element.113) | copy-start | bytes 6291460
  230.1 3.0 copy-start.22
  230.1 3.0 copy-start.61
  230.1 3.0 copy-start.75
  354.7 7.1 %copy-start.76 = (bf16[128,1024]{1,0:T(8,128)(2,1)S(1)}, bf16[128,1024]{1,0:T(8,128)(2,1)}, u32[]{:S(2)}) copy-start(bf16[128,1024]{1,0:T(8,128)(2,1)} %param.6) | copy-start | bytes 786436
  354.8 7.1 %copy-start.84 = (pred[512,128]{1,0:T(8,128)(4,1)S(1)}, pred[512,128]{1,0:T(8,128)(4,1)}, u32[]{:S(2)}) copy-start(pred[512,128]{1,0:T(8,128)(4,1)} %get-tuple-element.91) | copy-start | bytes 196612
  363.9 6.0 %copy-start.18 = (f32[8,512,128]{2,1,0:T(8,128)S(1)}, f32[8,512,128]{2,1,0:T(8,128)}, u32[]{:S(2)}) copy-start(f32[8,512,128]{2,1,0:T(8,128)} %select_exponential_fusion.7) | copy-start | bytes 6291460
  375.0 3.7 copy-start.47
  375.0 3.7 copy-start.77
  375.0 3.7 copy-start.83
  375.0 3.7 copy-start.89
  389.3 2.2 copy-start.17
  395.4 4.3 copy-start.14
  403.6 4.3 copy-start.12
  421.3 2.6 copy-start.16
  421.3 3.0 copy-start.40
  (63 other events, 107.9 us)
Sparse Core Ops, SparseCore 0:
  11.1 89.8 all-gather.4
  103.5 74.2 all-gather.6
  180.8 86.5 all-gather.8
  269.8 85.6 all-gather.10
where the time goes:
time: 447 us; the launch traced here: 441 us
  waiting for transfers between devices  152 us (34%)
  blocking collectives  95.1 us (21%)
  matrix products  91.7 us (21%)
  local copies, waits for them, and re-layouts  78.7 us (18%)
  between operations  14.9 us (3%)
  other arithmetic  8.3 us (2%)
    all_gather x1, waiting for transfers between devices, per_device(): piece_keys = lax.all_gather(key_rows, 'seq', axis=0, tiled=True)  84.6 us
    all_gather x1, waiting for transfers between devices, per_device(): piece_values = lax.all_gather(value_rows, 'seq', axis=0, tiled=True)  66.8 us
    all_gather x1, blocking collectives, per_device(): lax.all_gather(inner_sum, 'seq', axis=1, tiled=True)  47.9 us
    all_gather x1, blocking collectives, per_device(): lax.all_gather(log_norm, 'seq', axis=1, tiled=True)  47.2 us
    unnamed x189, local copies, waits for them, and re-layouts  36 us
    dot_general x8, matrix products, backward_update(): jnp.einsum('hqk,qhd->khd', score_grad.astype(jnp.bfloat16), block_queries...  31.8 us
    slice x9, local copies, waits for them, and re-layouts, per_device(): piece_values[offset:offset + block_size]  24.6 us
    dot_general x8, matrix products, backward_update(): jnp.einsum('qhd,khd->hqk', block_queries, key_heads, preferred_element_ty...  18.4 us
  transfers between devices with their start and end apart: 4, of which 2 were waited for; matrix products, arithmetic and copies ran while one was open for 20% of the time, Pallas kernels for 0%

commit v1 on v0

v1 whole, which is shorter than its diff:
```python
import functools
import math

import jax
import jax.numpy as jnp
from jax import lax
from jax.experimental import pallas as pl
from jax.experimental.pallas import tpu as pltpu
from jax.sharding import PartitionSpec as P

HEADS = 8
D = 128
TOK = 128
NX = 4
NZ = 4
COL = NZ * 2 * TOK
TOKENS = NX * COL
SCALES = 12
FACTOR = 1.0 / math.sqrt(D)
EXP2_FACTOR = FACTOR * math.log2(math.e)
NEG = -1e30
BIG = 1 << 30
MESH = pl.DeviceIdType.MESH
F32 = jnp.float32
BF16 = jnp.bfloat16
PARTNERS = (4, 5, 2, 3, 6, 7, 1)


def coords():
    s = lax.axis_index("seq")
    return s // 8, (s // 2) % 4, s % 2


def device(x, z, c):
    return (lax.axis_index("dp"), lax.rem(x, NX) * 8 + lax.rem(z, NZ) * 2 + lax.rem(c, 2))


def rows_of(start, size):
    return pl.ds(pl.multiple_of(start, TOK), size)


def dot(a, b):
    return jnp.dot(a, b, preferred_element_type=F32)


def barrier(x, z, c):
    sem = pltpu.get_barrier_semaphore()
    for i in PARTNERS:
        pl.semaphore_signal(sem, inc=1, device_id=device(x, z + i // 2, c + i % 2), device_id_type=MESH)
    for dx in (1, 3):
        pl.semaphore_signal(sem, inc=1, device_id=device(x + dx, z, c), device_id_type=MESH)
    pl.semaphore_wait(sem, len(PARTNERS) + 2)


def gather_kernel(q_ref, k_ref, v_ref, g_ref, qo, ko, vo, go, zs, zr, loc, xs, xr):
    x, z, c = coords()
    me = z * 2 + c
    barrier(x, z, c)
    base = x * COL
    plan = ((k_ref, ko, base), (v_ref, vo, base), (q_ref, qo, 0), (g_ref, go, 0))

    def z_copy(a, i):
        src, dst, off = plan[a]
        pz, pc = lax.rem(z + i // 2, NZ), lax.rem(c + i % 2, 2)
        there = dst.at[rows_of(off + me * TOK, TOK)]
        mine = src.at[:, pl.ds(pl.multiple_of((pz * 2 + pc) * D, D), D)]
        if i == 0:
            return pltpu.make_async_copy(mine, there, loc.at[a])
        return pltpu.make_async_remote_copy(
            src_ref=mine, dst_ref=there, send_sem=zs.at[a, i], recv_sem=zr.at[a, i],
            device_id=device(x, pz, pc), device_id_type=MESH,
        )

    zc = [[z_copy(a, i) for i in (0,) + PARTNERS] for a in range(4)]
    for copies in zc:
        for copy in copies:
            copy.start()

    HALF = COL // 2

    def x_copy(a, kind, dx, col, half):
        ref = (ko, vo)[a].at[rows_of(lax.rem(col, NX) * COL + half * HALF, HALF)]
        return pltpu.make_async_remote_copy(
            src_ref=ref, dst_ref=ref, send_sem=xs.at[a, kind], recv_sem=xr.at[a, kind],
            device_id=device(x + dx, z, c), device_id_type=MESH,
        )

    xc = []
    for a in range(2):
        for copy in zc[a]:
            copy.wait() if copy is zc[a][0] else copy.wait_recv()
        own = [x_copy(a, 0, 1, x, 0), x_copy(a, 1, 3, x, 1), x_copy(a, 2, 1, x, 1), x_copy(a, 3, 3, x, 0)]
        for copy in own:
            copy.start()
        xc.append(own)
    for a in range(2):
        own = xc[a]
        own[0].wait_recv()
        f0 = x_copy(a, 4, 1, x + 3, 0)
        f0.start()
        own[1].wait_recv()
        f1 = x_copy(a, 5, 3, x + 1, 1)
        f1.start()
        own += [f0, f1]
    for a in range(2):
        for n, copy in enumerate(xc[a]):
            if n >= 2:
                copy.wait_recv()
            copy.wait_send()
    for a in range(4):
        for copy in zc[a][1:]:
            if a >= 2:
                copy.wait_recv()
            copy.wait_send()
    for a in (2, 3):
        zc[a][0].wait()


def gather(q, k, v, g):
    small = jax.ShapeDtypeStruct((COL, D), BF16)
    large = jax.ShapeDtypeStruct((TOKENS, D), BF16)
    anyspace = pl.BlockSpec(memory_space=pl.ANY)
    return pl.pallas_call(
        gather_kernel,
        out_shape=(small, large, large, small),
        in_specs=[anyspace] * 4,
        out_specs=[anyspace] * 4,
        scratch_shapes=[
            pltpu.SemaphoreType.DMA((4, 8)),
            pltpu.SemaphoreType.DMA((4, 8)),
            pltpu.SemaphoreType.DMA((4,)),
            pltpu.SemaphoreType.DMA((2, 6)),
            pltpu.SemaphoreType.DMA((2, 6)),
        ],
        compiler_params=pltpu.CompilerParams(collective_id=0, has_side_effects=True),
        name="gather",
    )(q, k, v, g)


QB = 256
KB = 256


def attention_kernel(starts, q_ref, k_ref, v_ref, g_ref, o_ref, dq_ref, dk_ref, dv_ref,
                     qt, gt, kt, vt, pt, ot, ms, ls, gs, shr, ins, dqt):
    x, _, _ = coords()
    qt[:D, :] = q_ref[...].T
    gt[...] = g_ref[...].T
    for j in range(NX):
        rows = slice(j * COL, (j + 1) * COL)
        kt[:, rows] = k_ref[rows, :].T
        vt[:, rows] = v_ref[rows, :].T
    sub = lax.broadcasted_iota(jnp.int32, (D, COL), 0)
    pos = x * COL + lax.broadcasted_iota(jnp.int32, (D, COL), 1)
    nxt = jnp.full((D, COL), BIG, jnp.int32)
    now = jnp.full((D, COL), BIG, jnp.int32)
    lane = lax.broadcasted_iota(jnp.int32, (1, D), 1)
    starts_row = jnp.full((1, D), BIG, jnp.int32)
    for s in range(SCALES):
        nxt = jnp.where(sub == s, starts[s], nxt)
        now = jnp.where(sub == s + 1, starts[s], now)
        starts_row = jnp.where(lane == s, starts[s], starts_row)
    qt[D:, :] = jnp.where((nxt > pos) & (now <= pos), NEG, 0.0).astype(BF16)

    def scores(j, b):
        rows = pl.ds(pl.multiple_of(j * COL, COL), COL)
        cols = pl.ds(pl.multiple_of(b * QB, QB), QB)
        key_pos = j * COL + lax.broadcasted_iota(jnp.int32, (COL, D), 0)
        reached = jnp.where(key_pos >= starts_row, 1.0, 0.0).astype(BF16)
        s = dot(jnp.concatenate([k_ref[rows, :], reached], axis=1), qt[:, cols])
        m = jnp.max(s, axis=0, keepdims=True)
        p = jnp.exp2(s * EXP2_FACTOR - m * EXP2_FACTOR)
        ms[j, :, cols] = m * EXP2_FACTOR
        ls[j, :, cols] = jnp.sum(p, axis=0, keepdims=True)
        half = p.astype(BF16)
        pt[rows, cols] = half
        ot[j, :, cols] = dot(vt[:, rows], half)

    def first(n, carry):
        scores(n // (COL // QB), lax.rem(n, COL // QB))
        return carry

    lax.fori_loop(0, NX * (COL // QB), first, 0)

    top = jnp.maximum(jnp.maximum(ms[0], ms[1]), jnp.maximum(ms[2], ms[3]))
    shares = [jnp.exp2(ms[j] - top) for j in range(NX)]
    total = shares[0] * ls[0] + shares[1] * ls[1] + shares[2] * ls[2] + shares[3] * ls[3]
    inverse = 1.0 / total
    shares = [share * inverse for share in shares]
    o = ot[0] * shares[0] + ot[1] * shares[1] + ot[2] * shares[2] + ot[3] * shares[3]
    o_ref[...] = o.T.astype(BF16)
    g = gt[...].astype(F32)
    inner = jnp.sum(o * g, axis=0, keepdims=True)
    for j in range(NX):
        gs[j] = (g * shares[j]).T.astype(BF16)
        shr[j] = shares[j]
    ins[...] = inner
    dqt[...] = jnp.zeros_like(dqt)

    def second(n, carry):
        j = n // (COL // KB)
        rows = pl.ds(pl.multiple_of(n * KB, KB), KB)
        p = pt[rows, :]
        dp = dot(v_ref[rows, :], gt[...])
        ds = (p.astype(F32) * shr[j] * (dp - ins[...])).astype(BF16)
        dk_ref[rows, :] = (dot(ds, q_ref[...]) * FACTOR).astype(BF16)
        dv_ref[rows, :] = dot(p, gs[j]).astype(BF16)
        dqt[...] += dot(kt[:, rows], ds)
        return carry

    lax.fori_loop(0, TOKENS // KB, second, 0)
    dq_ref[...] = (dqt[...] * FACTOR).T.astype(BF16)


def attention(starts, q, k, v, g):
    small = jax.ShapeDtypeStruct((COL, D), BF16)
    large = jax.ShapeDtypeStruct((TOKENS, D), BF16)
    vm = pl.BlockSpec(memory_space=pltpu.VMEM)
    return pl.pallas_call(
        attention_kernel,
        out_shape=(small, small, large, large),
        in_specs=[pl.BlockSpec(memory_space=pltpu.SMEM)] + [vm] * 4,
        out_specs=[vm] * 4,
        scratch_shapes=[
            pltpu.VMEM((2 * D, COL), BF16),
            pltpu.VMEM((D, COL), BF16),
            pltpu.VMEM((D, TOKENS), BF16),
            pltpu.VMEM((D, TOKENS), BF16),
            pltpu.VMEM((TOKENS, COL), BF16),
            pltpu.VMEM((NX, D, COL), F32),
            pltpu.VMEM((NX, 1, COL), F32),
            pltpu.VMEM((NX, 1, COL), F32),
            pltpu.VMEM((NX, COL, D), BF16),
            pltpu.VMEM((NX, 1, COL), F32),
            pltpu.VMEM((1, COL), F32),
            pltpu.VMEM((D, COL), F32),
        ],
        compiler_params=pltpu.CompilerParams(vmem_limit_bytes=56 * 1024 * 1024),
        name="attention",
    )(starts, q, k, v, g)


def scatter_kernel(o_ref, dq_ref, dk_ref, dv_ref, oo, dqo, dko, dvo, land, mid, red, zs, zr, loc, xs, xr):
    x, z, c = coords()
    me = z * 2 + c
    barrier(x, z, c)
    HALF = COL // 2
    parts = (dk_ref, dv_ref)

    def x_copy(a, kind, dx, src, slot):
        return pltpu.make_async_remote_copy(
            src_ref=src, dst_ref=land.at[a, slot], send_sem=xs.at[a, kind], recv_sem=xr.at[a, kind],
            device_id=device(x + dx, z, c), device_id_type=MESH,
        )

    def part(a, col, half):
        return parts[a].at[rows_of(lax.rem(col, NX) * COL + half * HALF, HALF)]

    xc = []
    for a in range(2):
        own = [
            x_copy(a, 0, 1, part(a, x + 2, 0), 0),
            x_copy(a, 1, 3, part(a, x + 2, 1), 1),
            x_copy(a, 2, 1, part(a, x + 1, 1), 2),
            x_copy(a, 3, 3, part(a, x + 3, 0), 3),
        ]
        for copy in own:
            copy.start()
        xc.append(own)

    def z_copy(a, i):
        src = (o_ref, dq_ref, red.at[0], red.at[1])[a]
        dst = (oo, dqo, dko, dvo)[a]
        pz, pc = lax.rem(z + i // 2, NZ), lax.rem(c + i % 2, 2)
        there = dst.at[:, pl.ds(pl.multiple_of(me * D, D), D)]
        mine = src.at[rows_of((pz * 2 + pc) * TOK, TOK)]
        if i == 0:
            return pltpu.make_async_copy(mine, there, loc.at[a])
        return pltpu.make_async_remote_copy(
            src_ref=mine, dst_ref=there, send_sem=zs.at[a, i], recv_sem=zr.at[a, i],
            device_id=device(x, pz, pc), device_id_type=MESH,
        )

    zc = [[z_copy(a, i) for i in (0,) + PARTNERS] for a in range(4)]
    for copies in zc[:2]:
        for copy in copies:
            copy.start()
    for a in range(2):
        own = xc[a]
        own[0].wait_recv()
        mid[a, 0] = (land[a, 0].astype(F32) + part(a, x + 1, 0)[...].astype(F32)).astype(BF16)
        f0 = x_copy(a, 4, 1, mid.at[a, 0], 4)
        f0.start()
        own[1].wait_recv()
        mid[a, 1] = (land[a, 1].astype(F32) + part(a, x + 3, 1)[...].astype(F32)).astype(BF16)
        f1 = x_copy(a, 5, 3, mid.at[a, 1], 5)
        f1.start()
        own += [f0, f1]
    for a in range(2):
        own = xc[a]
        for copy in own[2:]:
            copy.wait_recv()
        red[a, :HALF] = (
            part(a, x, 0)[...].astype(F32) + land[a, 4].astype(F32) + land[a, 3].astype(F32)
        ).astype(BF16)
        red[a, HALF:] = (
            part(a, x, 1)[...].astype(F32) + land[a, 5].astype(F32) + land[a, 2].astype(F32)
        ).astype(BF16)
        for copy in zc[2 + a]:
            copy.start()
    for a in range(2):
        for copy in xc[a]:
            copy.wait_send()
    for copies in zc:
        for copy in copies:
            copy.wait()


def scatter(o, dq, dk, dv):
    out = jax.ShapeDtypeStruct((TOK, HEADS * D), BF16)
    anyspace = pl.BlockSpec(memory_space=pl.ANY)
    vm = pl.BlockSpec(memory_space=pltpu.VMEM)
    return pl.pallas_call(
        scatter_kernel,
        out_shape=(out,) * 4,
        in_specs=[anyspace, anyspace, vm, vm],
        out_specs=[anyspace] * 4,
        scratch_shapes=[
            pltpu.VMEM((2, 6, COL // 2, D), BF16),
            pltpu.VMEM((2, 2, COL // 2, D), BF16),
            pltpu.VMEM((2, COL, D), BF16),
            pltpu.SemaphoreType.DMA((4, 8)),
            pltpu.SemaphoreType.DMA((4, 8)),
            pltpu.SemaphoreType.DMA((4,)),
            pltpu.SemaphoreType.DMA((2, 6)),
            pltpu.SemaphoreType.DMA((2, 6)),
        ],
        compiler_params=pltpu.CompilerParams(
            collective_id=1, has_side_effects=True, vmem_limit_bytes=32 * 1024 * 1024
        ),
        name="scatter",
    )(o, dq, dk, dv)


def per_device(queries, key_rows, value_rows, out_cotangent, scale_starts):
    q, k, v, g = gather(queries, key_rows, value_rows, out_cotangent)
    o, dq, dk, dv = attention(scale_starts, q, k, v, g)
    return scatter(o, dq, dk, dv)


def solution(mesh):
    rows = P(("dp", "seq"), None)
    return jax.shard_map(
        per_device,
        mesh=mesh,
        in_specs=(rows, rows, rows, rows, P("dp")),
        out_specs=(rows,) * 4,
        check_vma=False,
    )
```

time: 447 us -> 109 us (0.24); the launches traced: 441 us -> 108 us
  waiting for transfers between devices: 152 us -> 0 us
  Pallas kernels: 0 us -> 101 us
  blocking collectives: 95.1 us -> 0 us
  matrix products: 91.7 us -> 0 us
  local copies, waits for them, and re-layouts: 78.7 us -> 7.16 us
  between operations: 14.9 us -> 0.65 us
  other arithmetic: 8.3 us -> 0 us
    all_gather x4 -> x0, waiting for transfers between devices: 151 us -> none  [the longest x1 84.6 us: per_device(): piece_keys = lax.all_gather(key_rows, 'seq', axis=0, tiled=True)]
    pallas_call x0 -> x3, Pallas kernels: none -> 101 us  [the longest x1 38.7 us: gather(): pl.pallas_call(gather_kernel, out_shape=(small, large, large, small), in_...]
    all_gather x2 -> x0, blocking collectives: 95.1 us -> none  [the longest x1 47.9 us: per_device(): lax.all_gather(inner_sum, 'seq', axis=1, tiled=True)]
    dot_general x64 -> x0, matrix products: 91.7 us -> none  [the longest x8 31.8 us: backward_update(): jnp.einsum('hqk,qhd->khd', score_grad.astype(jnp.bfloat16), block_queries...]
    slice x12 -> x0, local copies, waits for them, and re-layouts: 42 us -> none  [the longest x9 24.6 us: per_device(): piece_values[offset:offset + block_size]]
    unnamed x189 -> x12, local copies, waits for them, and re-layouts: 36 us -> 7.16 us
    reduce_sum x10 -> x0, other arithmetic: 5.73 us -> none  [the longest x8 5.51 us: stats_update(): jnp.sum(terms, axis=2)]
  transfers between devices with their start and end apart: 4 -> 0, of which waited for: 2 -> 0; matrix products, arithmetic and copies ran while one was open for 20% -> 0% of each run, Pallas kernels for 0% -> 0%
where the time goes in v1:
time: 109 us; the launch traced here: 108 us
  Pallas kernels  101 us (93%)
  local copies, waits for them, and re-layouts  7.16 us (7%)
    pallas_call x1, Pallas kernels, gather(): pl.pallas_call(gather_kernel, out_shape=(small, large, large, small), in_...  38.7 us
    pallas_call x1, Pallas kernels, scatter(): pl.pallas_call(scatter_kernel, out_shape=(out,) * 4, in_specs=[anyspace,...  34.6 us
    pallas_call x1, Pallas kernels, attention(): pl.pallas_call(attention_kernel, out_shape=(small, small, large, large),...  27.4 us
    unnamed x12, local copies, waits for them, and re-layouts  7.16 us

profile of v1, /device:TPU:1, one launch (start us, length us, event | category | flops | bytes accessed | tf_op | source)
XLA Modules:
  0.0 108.5 jit_solution(16930604584620384663)
XLA Ops:
  0.6 38.7 %gather.1 = (bf16[1024,128]{1,0:T(8,128)(2,1)}, bf16[4096,128]{1,0:T(8,128)(2,1)}, bf16[4096,128]{1,0:T(8,128)(2,1)}, bf16[1024,128]{1,0:T(8,128)(2,1)}) custom-call(bf16[128,1024]{1,0:T(8,128)(2,1)} %q_ref.1, bf16[128,1024]{1,0:T(8,128)(2,1)} %k_ref.1, bf16[128,1024]{1,0:T(8,128)(2,1)} %v_ref.1, bf16[128,1024]{1,0:T(8,128)(2,1)} %g_ref.1), custom_call_target="tpu_custom_call" | custom-call | tf_op jit(solution)/shard_map/gather/pallas_call | solution.py:123
  39.3 27.4 %attention.1 = (bf16[1024,128]{1,0:T(8,128)(2,1)}, bf16[1024,128]{1,0:T(8,128)(2,1)}, bf16[4096,128]{1,0:T(8,128)(2,1)}, bf16[4096,128]{1,0:T(8,128)(2,1)}) custom-call(s32[12]{0:T(128)} %starts.1, bf16[1024,128]{1,0:T(8,128)(2,1)} %get-tuple-element.12.q_ref, bf16[4096,128]{1,0:T(8,128)(2,1)} %get-tuple-element.13.k_ref, ...), custom_call_target="tpu_custom_call" | custom-call | tf_op jit(solution)/shard_map/attention/pallas_call | solution.py:219
  66.7 0.0 copy-start
  66.7 1.2 %copy-done = bf16[4096,128]{1,0:T(8,128)(2,1)S(1)} copy-done((bf16[4096,128]{1,0:T(8,128)(2,1)S(1)}, bf16[4096,128]{1,0:T(8,128)(2,1)}, u32[]{:S(2)}) %copy-start) | copy-done | bytes 1048600
  68.0 0.0 copy-start.1
  68.0 1.2 %copy-done.1 = bf16[4096,128]{1,0:T(8,128)(2,1)S(1)} copy-done((bf16[4096,128]{1,0:T(8,128)(2,1)S(1)}, bf16[4096,128]{1,0:T(8,128)(2,1)}, u32[]{:S(2)}) %copy-start.1) | copy-done | bytes 1048600
  69.2 0.0 copy-start.2
  69.2 0.9 copy-done.2
  70.1 0.0 copy-start.3
  70.1 0.9 copy-done.3
  71.1 34.6 %scatter.1 = (bf16[128,1024]{1,0:T(8,128)(2,1)S(1)}, bf16[128,1024]{1,0:T(8,128)(2,1)S(1)}, bf16[128,1024]{1,0:T(8,128)(2,1)S(1)}, bf16[128,1024]{1,0:T(8,128)(2,1)S(1)}) custom-call(bf16[1024,128]{1,0:T(8,128)(2,1)S(1)} %copy-done.2, bf16[1024,128]{1,0:T(8,128)(2,1)S(1)} %copy-done.3, bf16[4096,128]{1,0:T(8,128)(2,1)S(1)} %copy-done, ...), custom_call_target="tpu_custom_call" | custom-call | tf_op jit(solution)/shard_map/scatter/pallas_call | solution.py:323
  105.7 0.7 copy.13
  106.4 0.7 copy.14
  107.1 0.7 copy.15
  107.8 0.7 copy.16
Async XLA Ops:
  66.7 1.2 %copy-start = (bf16[4096,128]{1,0:T(8,128)(2,1)S(1)}, bf16[4096,128]{1,0:T(8,128)(2,1)}, u32[]{:S(2)}) copy-start(bf16[4096,128]{1,0:T(8,128)(2,1)} %get-tuple-element.18.dk_ref) | copy-start | bytes 3145732
  68.0 1.2 %copy-start.1 = (bf16[4096,128]{1,0:T(8,128)(2,1)S(1)}, bf16[4096,128]{1,0:T(8,128)(2,1)}, u32[]{:S(2)}) copy-start(bf16[4096,128]{1,0:T(8,128)(2,1)} %get-tuple-element.19.dv_ref) | copy-start | bytes 3145732
  69.2 0.9 copy-start.2
  70.1 0.9 copy-start.3

commit v2 on v1

v2 whole, which is shorter than its diff:
```python
import math

import jax
import jax.numpy as jnp
from jax import lax
from jax.experimental import pallas as pl
from jax.experimental.pallas import tpu as pltpu
from jax.sharding import PartitionSpec as P

HEADS = 8
D = 128
TOK = 128
NX = 4
NZ = 4
COL = NZ * 2 * TOK
HALF = COL // 2
SCALES = 12
QB = 512
FACTOR = 1.0 / math.sqrt(D)
EXP2_FACTOR = FACTOR * math.log2(math.e)
NEG = -1e30
BIG = 1 << 30
MESH = pl.DeviceIdType.MESH
F32 = jnp.float32
BF16 = jnp.bfloat16
PARTNERS = (4, 5, 2, 3, 6, 7, 1)
K, V, Q, G = range(4)
O, DQ, DK, DV = range(4, 8)


def dot(a, b):
    return jnp.dot(a, b, preferred_element_type=F32)


def wide(a):
    return a.astype(F32)


def fused_kernel(
    starts, q_ref, k_ref, v_ref, g_ref, oo, dqo, dko, dvo,
    qg, gg, kg, vg, qt, gt, kt, vt, pt, ot, ms, ls, gs, shr, ins, dqt, sbuf,
    part, land, mid, red, ob, dqb, zs, zr, loc, xs, xr, ys, yr,
):
    s = lax.axis_index("seq")
    x, z, c = s // 8, (s // 2) % 4, s % 2
    me = z * 2 + c

    def device(x, z, c):
        return (lax.axis_index("dp"), lax.rem(x, NX) * 8 + lax.rem(z, NZ) * 2 + lax.rem(c, 2))

    sem = pltpu.get_barrier_semaphore()
    for i in PARTNERS:
        pl.semaphore_signal(sem, inc=1, device_id=device(x, z + i // 2, c + i % 2), device_id_type=MESH)
    for dx in (1, 3):
        pl.semaphore_signal(sem, inc=1, device_id=device(x + dx, z, c), device_id_type=MESH)
    pl.semaphore_wait(sem, len(PARTNERS) + 2)

    def z_copy(a, i):
        pz, pc = lax.rem(z + i // 2, NZ), lax.rem(c + i % 2, 2)
        his = pz * 2 + pc
        if a < 4:
            src = (k_ref, v_ref, q_ref, g_ref)[a].at[:, pl.ds(pl.multiple_of(his * D, D), D)]
            dst = (kg.at[0], vg.at[0], qg, gg)[a].at[pl.ds(pl.multiple_of(me * TOK, TOK), TOK)]
        else:
            src = (ob, dqb, red.at[0], red.at[1])[a - 4].at[pl.ds(pl.multiple_of(his * TOK, TOK), TOK)]
            dst = (oo, dqo, dko, dvo)[a - 4].at[:, pl.ds(pl.multiple_of(me * D, D), D)]
        if i == 0:
            return pltpu.make_async_copy(src, dst, loc.at[a])
        return pltpu.make_async_remote_copy(
            src_ref=src, dst_ref=dst, send_sem=zs.at[a, i], recv_sem=zr.at[a, i],
            device_id=device(x, pz, pc), device_id_type=MESH,
        )

    def z_start(a):
        copies = [z_copy(a, i) for i in (0,) + PARTNERS]
        for copy in copies:
            copy.start()
        return copies

    def z_arrive(copies):
        copies[0].wait()
        for copy in copies[1:]:
            copy.wait_recv()

    def x_copy(sems, a, kind, dx, src, dst):
        copy = pltpu.make_async_remote_copy(
            src_ref=src, dst_ref=dst, send_sem=sems[0].at[a, kind], recv_sem=sems[1].at[a, kind],
            device_id=device(x + dx, z, c), device_id_type=MESH,
        )
        copy.start()
        return copy

    def spread(a, kind, dx, slot, half):
        ref = (kg, vg)[a]
        rows = pl.ds(half * HALF, HALF)
        return x_copy((xs, xr), a, kind, dx, ref.at[slot, rows], ref.at[(slot - dx) % NX, rows])

    zc = [z_start(a) for a in (K, V, Q, G)]

    sub = lax.broadcasted_iota(jnp.int32, (D, COL), 0)
    pos = x * COL + lax.broadcasted_iota(jnp.int32, (D, COL), 1)
    nxt = jnp.full((D, COL), BIG, jnp.int32)
    now = jnp.full((D, COL), BIG, jnp.int32)
    lane = lax.broadcasted_iota(jnp.int32, (1, D), 1)
    starts_row = jnp.full((1, D), BIG, jnp.int32)
    for n in range(SCALES):
        nxt = jnp.where(sub == n, starts[n], nxt)
        now = jnp.where(sub == n + 1, starts[n], now)
        starts_row = jnp.where(lane == n, starts[n], starts_row)
    qt[D:, :] = jnp.where((nxt > pos) & (now <= pos), NEG, 0.0).astype(BF16)

    xc = [None, None]
    for a in (K, V):
        z_arrive(zc[a])
        xc[a] = [spread(a, 0, 1, 0, 0), spread(a, 1, 3, 0, 1), spread(a, 2, 1, 0, 1), spread(a, 3, 3, 0, 0)]

    def forward(a):
        xc[a][0].wait_recv()
        xc[a].append(spread(a, 4, 1, 3, 0))
        xc[a][1].wait_recv()
        xc[a].append(spread(a, 5, 3, 1, 1))

    def transposed(a, slot):
        (kt, vt)[a][slot] = (kg, vg)[a][slot].T

    transposed(K, 0)
    transposed(V, 0)
    forward(K)
    xc[K][2].wait_recv()
    xc[K][3].wait_recv()
    transposed(K, 1)
    transposed(K, 3)
    z_arrive(zc[Q])
    qt[:D, :] = qg[...].T
    xc[K][4].wait_recv()
    xc[K][5].wait_recv()
    transposed(K, 2)

    def scores(n):
        slot, cols = n // 2, pl.ds(n % 2 * QB, QB)
        key_pos = lax.rem(x + slot, NX) * COL + lax.broadcasted_iota(jnp.int32, (COL, D), 0)
        reached = jnp.where(key_pos >= starts_row, 1.0, 0.0).astype(BF16)
        sbuf[n % 2] = dot(jnp.concatenate([kg[slot], reached], axis=1), qt[:, cols])

    def soften(n):
        slot, cols = n // 2, pl.ds(n % 2 * QB, QB)
        scored = sbuf[n % 2]
        m = jnp.max(scored, axis=0, keepdims=True) * EXP2_FACTOR
        p = jnp.exp2(scored * EXP2_FACTOR - m)
        ms[slot, :, cols] = m
        ls[slot, :, cols] = jnp.sum(p, axis=0, keepdims=True)
        half = p.astype(BF16)
        pt[slot, :, cols] = half
        ot[slot, :, cols] = dot(vt[slot], half)

    order = (0, 1, 6, 7, 2, 3, 4, 5)

    def first(begin, end):
        for n in range(begin, end):
            if n + 1 < len(order):
                scores(order[n + 1])
            soften(order[n])

    scores(order[0])
    first(0, 2)
    forward(V)
    xc[V][2].wait_recv()
    xc[V][3].wait_recv()
    transposed(V, 1)
    transposed(V, 3)
    first(2, 6)
    xc[V][4].wait_recv()
    xc[V][5].wait_recv()
    transposed(V, 2)
    first(6, 8)

    z_arrive(zc[G])
    gt[...] = gg[...].T
    top = jnp.maximum(jnp.maximum(ms[0], ms[1]), jnp.maximum(ms[2], ms[3]))
    shares = [jnp.exp2(ms[j] - top) for j in range(NX)]
    inverse = 1.0 / (shares[0] * ls[0] + shares[1] * ls[1] + shares[2] * ls[2] + shares[3] * ls[3])
    shares = [share * inverse for share in shares]
    o = ot[0] * shares[0] + ot[1] * shares[1] + ot[2] * shares[2] + ot[3] * shares[3]
    ob[...] = o.T.astype(BF16)
    zc.append(z_start(O))
    g = wide(gt[...])
    ins[...] = jnp.sum(o * g, axis=0, keepdims=True)
    for j in range(NX):
        gs[j] = (g * shares[j]).T.astype(BF16)
        shr[j] = shares[j]

    def second(slot):
        p = pt[slot]
        ds = (wide(p) * shr[slot] * (dot(vg[slot], gt[...]) - ins[...])).astype(BF16)
        part[0, slot] = (dot(ds, qg[...]) * FACTOR).astype(BF16)
        part[1, slot] = dot(p, gs[slot]).astype(BF16)
        more = dot(kt[slot], ds)
        dqt[...] = more if slot == 2 else dqt[...] + more

    def collect(a, kind, dx, src):
        return x_copy((ys, yr), a, kind, dx, src, land.at[a, kind])

    low, high = pl.ds(0, HALF), pl.ds(HALF, HALF)
    yc = [[None] * 6, [None] * 6]
    second(2)
    for a in range(2):
        yc[a][0] = collect(a, 0, 1, part.at[a, 2, low])
        yc[a][1] = collect(a, 1, 3, part.at[a, 2, high])
    second(1)
    for a in range(2):
        yc[a][2] = collect(a, 2, 1, part.at[a, 1, high])
    second(3)
    for a in range(2):
        yc[a][3] = collect(a, 3, 3, part.at[a, 3, low])
    second(0)
    dqb[...] = (dqt[...] * FACTOR).T.astype(BF16)
    zc.append(z_start(DQ))
    for a in range(2):
        yc[a][0].wait_recv()
        mid[a, 0] = (wide(land[a, 0]) + wide(part[a, 1, low])).astype(BF16)
        yc[a][4] = collect(a, 4, 1, mid.at[a, 0])
        yc[a][1].wait_recv()
        mid[a, 1] = (wide(land[a, 1]) + wide(part[a, 3, high])).astype(BF16)
        yc[a][5] = collect(a, 5, 3, mid.at[a, 1])
    for a in range(2):
        for copy in yc[a][2:]:
            copy.wait_recv()
        red[a, low] = (wide(part[a, 0, low]) + wide(land[a, 4]) + wide(land[a, 3])).astype(BF16)
        red[a, high] = (wide(part[a, 0, high]) + wide(land[a, 5]) + wide(land[a, 2])).astype(BF16)
        zc.append(z_start(DK + a))
    for copies in xc + yc:
        for copy in copies:
            copy.wait_send()
    for a in range(8):
        if a >= 4:
            z_arrive(zc[a])
        for copy in zc[a][1:]:
            copy.wait_send()


def fused(starts, q, k, v, g):
    out = jax.ShapeDtypeStruct((TOK, HEADS * D), BF16)
    anyspace = pl.BlockSpec(memory_space=pl.ANY)
    dma = pltpu.SemaphoreType.DMA
    return pl.pallas_call(
        fused_kernel,
        out_shape=(out,) * 4,
        in_specs=[pl.BlockSpec(memory_space=pltpu.SMEM)] + [anyspace] * 4,
        out_specs=[anyspace] * 4,
        scratch_shapes=[
            pltpu.VMEM((COL, D), BF16),
            pltpu.VMEM((COL, D), BF16),
            pltpu.VMEM((NX, COL, D), BF16),
            pltpu.VMEM((NX, COL, D), BF16),
            pltpu.VMEM((2 * D, COL), BF16),
            pltpu.VMEM((D, COL), BF16),
            pltpu.VMEM((NX, D, COL), BF16),
            pltpu.VMEM((NX, D, COL), BF16),
            pltpu.VMEM((NX, COL, COL), BF16),
            pltpu.VMEM((NX, D, COL), F32),
            pltpu.VMEM((NX, 1, COL), F32),
            pltpu.VMEM((NX, 1, COL), F32),
            pltpu.VMEM((NX, COL, D), BF16),
            pltpu.VMEM((NX, 1, COL), F32),
            pltpu.VMEM((1, COL), F32),
            pltpu.VMEM((D, COL), F32),
            pltpu.VMEM((2, COL, QB), F32),
            pltpu.VMEM((2, NX, COL, D), BF16),
            pltpu.VMEM((2, 6, HALF, D), BF16),
            pltpu.VMEM((2, 2, HALF, D), BF16),
            pltpu.VMEM((2, COL, D), BF16),
            pltpu.VMEM((COL, D), BF16),
            pltpu.VMEM((COL, D), BF16),
            dma((8, 8)),
            dma((8, 8)),
            dma((8,)),
            dma((2, 6)),
            dma((2, 6)),
            dma((2, 6)),
            dma((2, 6)),
        ],
        compiler_params=pltpu.CompilerParams(
            collective_id=0, has_side_effects=True, vmem_limit_bytes=58 * 1024 * 1024
        ),
        name="fused",
    )(starts, q, k, v, g)


def per_device(queries, key_rows, value_rows, out_cotangent, scale_starts):
    return fused(scale_starts, queries, key_rows, value_rows, out_cotangent)


def solution(mesh):
    rows = P(("dp", "seq"), None)
    return jax.shard_map(
        per_device,
        mesh=mesh,
        in_specs=(rows, rows, rows, rows, P("dp")),
        out_specs=(rows,) * 4,
        check_vma=False,
    )
```

time: 109 us -> 83.5 us (0.77)
  Pallas kernels: 101 us -> 78.1 us
  local copies, waits for them, and re-layouts: 7.16 us -> 4.5 us
    pallas_call x3 -> x1, Pallas kernels: 101 us -> 78.1 us  [fused(): pl.pallas_call(fused_kernel, out_shape=(out,) * 4, in_specs=[pl.BlockSpec...]
    unnamed x12 -> x10, local copies, waits for them, and re-layouts: 7.16 us -> 4.5 us
where the time goes in v2:
time: 83.5 us; the launch traced here: 83.3 us
  Pallas kernels  78.1 us (94%)
  local copies, waits for them, and re-layouts  4.5 us (5%)
    pallas_call x1, Pallas kernels, fused(): pl.pallas_call(fused_kernel, out_shape=(out,) * 4, in_specs=[pl.BlockSpec...  78.1 us
    unnamed x10, local copies, waits for them, and re-layouts  4.5 us

profile of v2, /device:TPU:1, one launch (start us, length us, event | category | flops | bytes accessed | tf_op | source)
XLA Modules:
  0.0 83.3 jit_solution(13977013877077098240)
XLA Ops:
  0.6 78.1 %fused.1 = (bf16[128,1024]{1,0:T(8,128)(2,1)}, bf16[128,1024]{1,0:T(8,128)(2,1)}, bf16[128,1024]{1,0:T(8,128)(2,1)}, bf16[128,1024]{1,0:T(8,128)(2,1)}) custom-call(s32[12]{0:T(128)} %starts.1, bf16[128,1024]{1,0:T(8,128)(2,1)} %q_ref.1, bf16[128,1024]{1,0:T(8,128)(2,1)} %k_ref.1, bf16[128,1024]{1,0:T(8,128)(2,1)} %v_ref.1, bf16[128,1024]{1,0:T(8,128)(2,1)} %g_ref.1), custom_call_target="tpu_custom_call" | custom-call | tf_op jit(solution)/shard_map/fused/pallas_call | solution.py:245
  78.8 0.0 copy-start.2
  78.8 1.7 %copy.13 = bf16[128,1024]{1,0:T(8,128)(2,1)} copy(bf16[128,1024]{1,0:T(8,128)(2,1)} %get-tuple-element.8) | data formatting | bytes 524288
  80.5 0.0 copy-done.2
  80.5 0.0 copy-start.1
  80.5 0.7 copy.14
  81.2 0.3 copy-done.1
  81.5 0.0 copy-start
  81.5 0.7 copy.15
  82.2 0.3 copy-done
  82.6 0.7 copy.16
Async XLA Ops:
  78.8 1.7 %copy-start.2 = (bf16[128,1024]{1,0:T(8,128)(2,1)S(1)}, bf16[128,1024]{1,0:T(8,128)(2,1)}, u32[]{:S(2)}) copy-start(bf16[128,1024]{1,0:T(8,128)(2,1)} %get-tuple-element.9) | copy-start | bytes 786436
  80.5 1.0 %copy-start.1 = (bf16[128,1024]{1,0:T(8,128)(2,1)S(1)}, bf16[128,1024]{1,0:T(8,128)(2,1)}, u32[]{:S(2)}) copy-start(bf16[128,1024]{1,0:T(8,128)(2,1)} %get-tuple-element.10) | copy-start | bytes 786436
  81.5 1.0 %copy-start = (bf16[128,1024]{1,0:T(8,128)(2,1)S(1)}, bf16[128,1024]{1,0:T(8,128)(2,1)}, u32[]{:S(2)}) copy-start(bf16[128,1024]{1,0:T(8,128)(2,1)} %get-tuple-element.11) | copy-start | bytes 786436

commit v3 on v2

v3 whole, which is shorter than its diff:
```python
import math

import jax
import jax.numpy as jnp
from jax import lax
from jax.experimental import pallas as pl
from jax.experimental.pallas import tpu as pltpu
from jax.sharding import PartitionSpec as P

HEADS = 8
D = 128
TOK = 128
NX = 4
NZ = 4
COL = NZ * 2 * TOK
SCALES = 12
QB = 512
FACTOR = 1.0 / math.sqrt(D)
EXP2_FACTOR = FACTOR * math.log2(math.e)
NEG = -1e30
BIG = 1 << 30
MESH = pl.DeviceIdType.MESH
F32 = jnp.float32
BF16 = jnp.bfloat16
PIECES = (4, 5, 2, 3, 6, 7, 1, 0)
NEAR, FAR = (2, 3, 6, 7, 1, 0), (4, 5)
HALF = COL // 2
K, V, Q, G = range(4)
O, DQ, DV, DK = range(4, 8)


def dot(a, b):
    return jnp.dot(a, b, preferred_element_type=F32)


def wide(a):
    return a.astype(F32)


def fused_kernel(
    starts, q_ref, k_ref, v_ref, g_ref, oo, dqo, dvo, dko,
    qg, gg, kg, vg, qt, gt, kt, vt, pt, ot, ms, ls, gs, shr, ins, dqt, sbuf,
    part, land, mid, red, ob, dqb, zs, zr, xs, xr, ys, yr,
):
    s = lax.axis_index("seq")
    x, z, c = s // 8, (s // 2) % 4, s % 2
    p = x // 2
    guest = (c + p) % 2
    col = x + guest * (3 - 2 * x)
    head = 2 * z + p
    me = c * NZ + z

    def device(x, z, c):
        return (lax.axis_index("dp"), x * 8 + lax.rem(z, NZ) * 2 + lax.rem(c, 2))

    next_x = x + 1 - 2 * (x % 2)
    x_mate, d_mate = device(next_x, z, c), device(x, z, c + 1)
    sem = pltpu.get_barrier_semaphore()
    greeted = [device(x, z + i // 2, c + i % 2) for i in range(1, 8)]
    greeted += [device(3 - x, z + i // 2, c + i % 2) for i in range(8)] + [x_mate]
    for other in greeted:
        pl.semaphore_signal(sem, inc=1, device_id=other, device_id_type=MESH)
    pl.semaphore_wait(sem, len(greeted))

    def z_copy(a, i, local=False):
        far, one = lax.rem(z + i // 2, NZ), i % 2
        if a < 4:
            at = (far * 2 + (p + one) % 2) * D
            src = (k_ref, v_ref, q_ref, g_ref)[a].at[:, pl.ds(pl.multiple_of(at, D), D)]
            dst = (kg.at[0], vg.at[0], qg, gg)[a].at[pl.ds(pl.multiple_of(me * TOK, TOK), TOK)]
            there, kind = device(x + one * (3 - 2 * x), far, p), i // 2 * 2 + c
        else:
            at = (one * NZ + far) * TOK
            src = (ob, dqb, red.at[0], red.at[1])[a - 4].at[pl.ds(pl.multiple_of(at, TOK), TOK)]
            dst = (oo, dqo, dvo, dko)[a - 4].at[:, pl.ds(pl.multiple_of(head * D, D), D)]
            there, kind = device(col, far, one), i // 2 * 2 + guest
        if local:
            return pltpu.make_async_copy(src, dst, zr.at[a, kind])
        return pltpu.make_async_remote_copy(
            src_ref=src, dst_ref=dst, send_sem=zs.at[a, i], recv_sem=zr.at[a, kind],
            device_id=there, device_id_type=MESH,
        )

    def mine(a, i):
        if i > 1 or (i > 0 and a < 4):
            return None
        return (1 - guest) * (1 if a < 4 else 1 - (c + i) % 2) == 1

    def z_start(a, pieces=PIECES):
        for i in pieces:
            own = mine(a, i)
            if own is None:
                z_copy(a, i).start()
            else:
                pl.when(own)(lambda: z_copy(a, i, local=True).start())
                pl.when(jnp.logical_not(own))(lambda: z_copy(a, i).start())

    def z_arrive(a, pieces=PIECES):
        for i in pieces:
            if a < 4:
                dst = (kg.at[0], vg.at[0], qg, gg)[a].at[pl.ds(0, TOK)]
            else:
                dst = (oo, dqo, dvo, dko)[a - 4].at[:, pl.ds(0, D)]
            pltpu.make_async_copy(dst, dst, zr.at[a, i]).wait()

    def z_sent(a):
        for i in PIECES:
            own = mine(a, i)
            if own is None:
                z_copy(a, i).wait_send()
            else:
                pl.when(jnp.logical_not(own))(lambda: z_copy(a, i).wait_send())

    def to(mate, sems, a, kind, src, dst):
        copy = pltpu.make_async_remote_copy(
            src_ref=src, dst_ref=dst, send_sem=sems[0].at[a, kind], recv_sem=sems[1].at[a, kind],
            device_id=mate, device_id_type=MESH,
        )
        copy.start()
        return copy

    places = (col, col + 1 - 2 * (col % 2), 3 - col, 2 - col + 2 * (col % 2))

    def position(rows):
        return (rows >> 7 & 3) * 256 + (rows >> 9) * 128 + (rows & 127)

    z_start(K)
    z_start(V)

    sub = lax.broadcasted_iota(jnp.int32, (D, COL), 0)
    pos = col * COL + position(lax.broadcasted_iota(jnp.int32, (D, COL), 1))
    nxt = jnp.full((D, COL), BIG, jnp.int32)
    now = jnp.full((D, COL), BIG, jnp.int32)
    lane = lax.broadcasted_iota(jnp.int32, (1, D), 1)
    starts_row = jnp.full((1, D), BIG, jnp.int32)
    for n in range(SCALES):
        nxt = jnp.where(sub == n, starts[n], nxt)
        now = jnp.where(sub == n + 1, starts[n], now)
        starts_row = jnp.where(lane == n, starts[n], starts_row)
    qt[D:, :] = jnp.where((nxt > pos) & (now <= pos), NEG, 0.0).astype(BF16)

    xc = [None, None]

    def spread(a):
        z_arrive(a)
        ref = (kg, vg)[a]
        xc[a] = [to(x_mate, (xs, xr), a, 0, ref.at[0], ref.at[1]), to(d_mate, (xs, xr), a, 1, ref.at[0], ref.at[2])]

    def forward(a):
        ref = (kg, vg)[a]
        xc[a][0].wait_recv()
        xc[a].append(to(d_mate, (xs, xr), a, 2, ref.at[1], ref.at[3]))

    def transposed(a, slot):
        (kt, vt)[a][slot] = (kg, vg)[a][slot].T

    spread(K)
    z_start(Q)
    transposed(K, 0)
    spread(V)
    transposed(V, 0)
    xc[K][1].wait_recv()
    transposed(K, 2)
    forward(K)
    transposed(K, 1)
    xc[V][1].wait_recv()
    transposed(V, 2)
    z_arrive(Q, NEAR)
    z_start(G)
    z_arrive(Q, FAR)
    qt[:D, :] = qg[...].T
    xc[K][2].wait_recv()
    transposed(K, 3)

    def scores(n):
        slot, cols = n // 2, pl.ds(n % 2 * QB, QB)
        key_pos = places[slot] * COL + position(lax.broadcasted_iota(jnp.int32, (COL, D), 0))
        reached = jnp.where(key_pos >= starts_row, 1.0, 0.0).astype(BF16)
        sbuf[n % 2] = dot(jnp.concatenate([kg[slot], reached], axis=1), qt[:, cols])

    def soften(n):
        slot, cols = n // 2, pl.ds(n % 2 * QB, QB)
        scored = sbuf[n % 2]
        m = jnp.max(scored, axis=0, keepdims=True) * EXP2_FACTOR
        p = jnp.exp2(scored * EXP2_FACTOR - m)
        ms[slot, :, cols] = m
        ls[slot, :, cols] = jnp.sum(p, axis=0, keepdims=True)
        half = p.astype(BF16)
        pt[slot, :, cols] = half
        ot[slot, :, cols] = dot(vt[slot], half)

    order = (0, 1, 4, 5, 2, 3, 6, 7)

    def first(begin, end):
        for n in range(begin, end):
            if n + 1 < len(order):
                scores(order[n + 1])
            soften(order[n])

    scores(order[0])
    first(0, 3)
    forward(V)
    transposed(V, 1)
    first(3, 6)
    xc[V][2].wait_recv()
    transposed(V, 3)
    first(6, 8)

    top = jnp.maximum(jnp.maximum(ms[0], ms[1]), jnp.maximum(ms[2], ms[3]))
    shares = [jnp.exp2(ms[j] - top) for j in range(NX)]
    inverse = 1.0 / (shares[0] * ls[0] + shares[1] * ls[1] + shares[2] * ls[2] + shares[3] * ls[3])
    shares = [share * inverse for share in shares]
    o = ot[0] * shares[0] + ot[1] * shares[1] + ot[2] * shares[2] + ot[3] * shares[3]
    ot[0] = o
    ob[...] = o.astype(BF16).T
    z_start(O)
    for j in range(NX):
        shr[j] = shares[j]
    z_arrive(G)
    gt[...] = gg[...].T

    def scaled(slot):
        gs[slot] = (wide(gt[...]) * shr[slot]).astype(BF16).T

    def second(slot):
        ds = (wide(pt[slot]) * shr[slot] * (dot(vg[slot], gt[...]) - ins[...])).astype(BF16)
        part[1, slot] = (dot(ds, qg[...]) * FACTOR).astype(BF16)
        more = dot(kt[slot], ds)
        dqt[...] = more if slot == 3 else dqt[...] + more

    yc = [[None] * 4, [None] * 4]

    def to_core(a, kind, slot):
        yc[a][kind] = to(d_mate, (ys, yr), a, kind, part.at[a, slot], land.at[a, kind])

    def to_chip(a):
        yc[a][0].wait_recv()
        for half in range(2):
            rows = pl.ds(half * HALF, HALF)
            mid[a, rows] = (wide(part[a, 1, rows]) + wide(land[a, 0, rows])).astype(BF16)
            yc[a][2 + half] = to(x_mate, (ys, yr), a, 2 + half, mid.at[a, rows], land.at[a, 2, rows])

    def total(a):
        for half in range(2):
            rows = pl.ds(half * HALF, HALF)
            if half == 0:
                yc[a][1].wait_recv()
            yc[a][2 + half].wait_recv()
            red[a, rows] = (wide(part[a, 0, rows]) + wide(land[a, 1, rows]) + wide(land[a, 2, rows])).astype(BF16)
            z_start(DV + a, [i for i in PIECES if i % 2 == half])

    def value_part(slot):
        scaled(slot)
        part[0, slot] = dot(pt[slot], gs[slot]).astype(BF16)

    value_part(3)
    to_core(0, 0, 3)
    value_part(1)
    to_chip(0)
    value_part(2)
    to_core(0, 1, 2)
    value_part(0)
    ins[...] = jnp.sum(ot[0] * wide(gt[...]), axis=0, keepdims=True)
    second(3)
    to_core(1, 0, 3)
    second(1)
    to_chip(1)
    total(0)
    second(2)
    to_core(1, 1, 2)
    second(0)
    dqb[...] = (dqt[...] * FACTOR).astype(BF16).T
    z_start(DQ)
    total(1)
    for copies in xc + yc:
        for copy in copies:
            copy.wait_send()
    for a in range(4, 8):
        z_arrive(a)
    for a in range(8):
        z_sent(a)


def fused(starts, q, k, v, g):
    out = jax.ShapeDtypeStruct((TOK, HEADS * D), BF16)
    anyspace = pl.BlockSpec(memory_space=pl.ANY)
    dma = pltpu.SemaphoreType.DMA
    return pl.pallas_call(
        fused_kernel,
        out_shape=(out,) * 4,
        in_specs=[pl.BlockSpec(memory_space=pltpu.SMEM)] + [anyspace] * 4,
        out_specs=[anyspace] * 4,
        scratch_shapes=[
            pltpu.VMEM((COL, D), BF16),
            pltpu.VMEM((COL, D), BF16),
            pltpu.VMEM((NX, COL, D), BF16),
            pltpu.VMEM((NX, COL, D), BF16),
            pltpu.VMEM((2 * D, COL), BF16),
            pltpu.VMEM((D, COL), BF16),
            pltpu.VMEM((NX, D, COL), BF16),
            pltpu.VMEM((NX, D, COL), BF16),
            pltpu.VMEM((NX, COL, COL), BF16),
            pltpu.VMEM((NX, D, COL), F32),
            pltpu.VMEM((NX, 1, COL), F32),
            pltpu.VMEM((NX, 1, COL), F32),
            pltpu.VMEM((NX, COL, D), BF16),
            pltpu.VMEM((NX, 1, COL), F32),
            pltpu.VMEM((1, COL), F32),
            pltpu.VMEM((D, COL), F32),
            pltpu.VMEM((2, COL, QB), F32),
            pltpu.VMEM((2, NX, COL, D), BF16),
            pltpu.VMEM((2, 3, COL, D), BF16),
            pltpu.VMEM((2, COL, D), BF16),
            pltpu.VMEM((2, COL, D), BF16),
            pltpu.VMEM((COL, D), BF16),
            pltpu.VMEM((COL, D), BF16),
            dma((8, 8)),
            dma((8, 8)),
            dma((2, 3)),
            dma((2, 3)),
            dma((2, 4)),
            dma((2, 4)),
        ],
        compiler_params=pltpu.CompilerParams(
            collective_id=0, has_side_effects=True, vmem_limit_bytes=58 * 1024 * 1024
        ),
        name="fused",
    )(starts, q, k, v, g)


def handed_on_kernel(*refs):
    for n in range(4):
        refs[4 + n][...] = refs[n][...]


def handed_on(*arrays):
    vm = pl.BlockSpec(memory_space=pltpu.VMEM)
    return pl.pallas_call(
        handed_on_kernel,
        out_shape=tuple(jax.ShapeDtypeStruct(a.shape, a.dtype) for a in arrays),
        in_specs=[vm] * 4,
        out_specs=[vm] * 4,
        name="handed_on",
    )(*arrays)


def per_device(queries, key_rows, value_rows, out_cotangent, scale_starts):
    attended, query_grad, value_grad, key_grad = fused(scale_starts, queries, key_rows, value_rows, out_cotangent)
    return handed_on(attended, query_grad, key_grad, value_grad)


def solution(mesh):
    rows = P(("dp", "seq"), None)
    return jax.shard_map(
        per_device,
        mesh=mesh,
        in_specs=(rows, rows, rows, rows, P("dp")),
        out_specs=(rows,) * 4,
        check_vma=False,
    )
```

time: 83.5 us -> 72.4 us (0.87)
  Pallas kernels: 78.1 us -> 71.6 us
  local copies, waits for them, and re-layouts: 4.5 us -> 0 us
    pallas_call x1, Pallas kernels: 78.1 us -> 69.5 us  [fused(): pl.pallas_call(fused_kernel, out_shape=(out,) * 4, in_specs=[pl.BlockSpec...]
    unnamed x10 -> x0, local copies, waits for them, and re-layouts: 4.5 us -> none
    pallas_call x0 -> x1, Pallas kernels: none -> 2.17 us  [handed_on(): pl.pallas_call(handed_on_kernel, out_shape=tuple((jax.ShapeDtypeStruct(a....]
where the time goes in v3:
time: 72.4 us; the launch traced here: 72.3 us
  Pallas kernels  71.6 us (99%)
    pallas_call x1, Pallas kernels, fused(): pl.pallas_call(fused_kernel, out_shape=(out,) * 4, in_specs=[pl.BlockSpec...  69.5 us
    pallas_call x1, Pallas kernels, handed_on(): pl.pallas_call(handed_on_kernel, out_shape=tuple((jax.ShapeDtypeStruct(a....  2.17 us

profile of v3, /device:TPU:1, one launch (start us, length us, event | category | flops | bytes accessed | tf_op | source)
XLA Modules:
  0.0 72.3 jit_solution(14232466489191857834)
XLA Ops:
  0.6 69.5 %fused.1 = (bf16[128,1024]{1,0:T(8,128)(2,1)}, bf16[128,1024]{1,0:T(8,128)(2,1)}, bf16[128,1024]{1,0:T(8,128)(2,1)}, bf16[128,1024]{1,0:T(8,128)(2,1)}) custom-call(s32[12]{0:T(128)} %starts.1, bf16[128,1024]{1,0:T(8,128)(2,1)} %q_ref.1, bf16[128,1024]{1,0:T(8,128)(2,1)} %k_ref.1, bf16[128,1024]{1,0:T(8,128)(2,1)} %v_ref.1, bf16[128,1024]{1,0:T(8,128)(2,1)} %g_ref.1), custom_call_target="tpu_custom_call" | custom-call | tf_op jit(solution)/shard_map/fused/pallas_call | solution.py:288
  70.1 2.2 %handed_on.1 = (bf16[128,1024]{1,0:T(8,128)(2,1)}, bf16[128,1024]{1,0:T(8,128)(2,1)}, bf16[128,1024]{1,0:T(8,128)(2,1)}, bf16[128,1024]{1,0:T(8,128)(2,1)}) custom-call(bf16[128,1024]{1,0:T(8,128)(2,1)} %get-tuple-element.8.refs_0_, bf16[128,1024]{1,0:T(8,128)(2,1)} %get-tuple-element.9.refs_1_, bf16[128,1024]{1,0:T(8,128)(2,1)} %get-tuple-element.10.refs_2_, ...), custom_call_target="tpu_custom_call" | custom-call | tf_op jit(solution)/shard_map/handed_on/pallas_call | solution.py:338

commit v4 on v3

--- a/solution.py
+++ b/solution.py
@@ -23,6 +23,7 @@
 F32 = jnp.float32
 BF16 = jnp.bfloat16
 PIECES = (4, 5, 2, 3, 6, 7, 1, 0)
+INWARD = (5, 4, 3, 7, 2, 6, 1, 0)
 NEAR, FAR = (2, 3, 6, 7, 1, 0), (4, 5)
 HALF = COL // 2
 K, V, Q, G = range(4)
@@ -68,16 +69,17 @@
             at = (far * 2 + (p + one) % 2) * D
             src = (k_ref, v_ref, q_ref, g_ref)[a].at[:, pl.ds(pl.multiple_of(at, D), D)]
             dst = (kg.at[0], vg.at[0], qg, gg)[a].at[pl.ds(pl.multiple_of(me * TOK, TOK), TOK)]
-            there, kind = device(x + one * (3 - 2 * x), far, p), i // 2 * 2 + c
+            there = device(x + one * (3 - 2 * x), far, p)
         else:
             at = (one * NZ + far) * TOK
             src = (ob, dqb, red.at[0], red.at[1])[a - 4].at[pl.ds(pl.multiple_of(at, TOK), TOK)]
             dst = (oo, dqo, dvo, dko)[a - 4].at[:, pl.ds(pl.multiple_of(head * D, D), D)]
-            there, kind = device(col, far, one), i // 2 * 2 + guest
+            there = device(col, far, one)
+        kind = 0 if i in FAR else 1
         if local:
             return pltpu.make_async_copy(src, dst, zr.at[a, kind])
         return pltpu.make_async_remote_copy(
-            src_ref=src, dst_ref=dst, send_sem=zs.at[a, i], recv_sem=zr.at[a, kind],
+            src_ref=src, dst_ref=dst, send_sem=zs.at[a, kind], recv_sem=zr.at[a, kind],
             device_id=there, device_id_type=MESH,
         )
 
@@ -87,7 +89,7 @@
         return (1 - guest) * (1 if a < 4 else 1 - (c + i) % 2) == 1
 
     def z_start(a, pieces=PIECES):
-        for i in pieces:
+        for i in INWARD if a < 4 else pieces:
             own = mine(a, i)
             if own is None:
                 z_copy(a, i).start()
@@ -95,21 +97,20 @@
                 pl.when(own)(lambda: z_copy(a, i, local=True).start())
                 pl.when(jnp.logical_not(own))(lambda: z_copy(a, i).start())
 
+    def pieces_wait(sem, count):
+        block = red.at[0, pl.ds(0, count * TOK)]
+        pltpu.make_async_copy(block, block, sem).wait()
+
     def z_arrive(a, pieces=PIECES):
-        for i in pieces:
-            if a < 4:
-                dst = (kg.at[0], vg.at[0], qg, gg)[a].at[pl.ds(0, TOK)]
-            else:
-                dst = (oo, dqo, dvo, dko)[a - 4].at[:, pl.ds(0, D)]
-            pltpu.make_async_copy(dst, dst, zr.at[a, i]).wait()
+        if FAR[0] in pieces:
+            pieces_wait(zr.at[a, 0], len(FAR))
+        if NEAR[0] in pieces:
+            pieces_wait(zr.at[a, 1], len(NEAR))
 
     def z_sent(a):
-        for i in PIECES:
-            own = mine(a, i)
-            if own is None:
-                z_copy(a, i).wait_send()
-            else:
-                pl.when(jnp.logical_not(own))(lambda: z_copy(a, i).wait_send())
+        pieces_wait(zs.at[a, 0], len(FAR))
+        pieces_wait(zs.at[a, 1], len(NEAR) - 1)
+        pl.when(guest == 1)(lambda: pieces_wait(zs.at[a, 1], 1))
 
     def to(mate, sems, a, kind, src, dst):
         copy = pltpu.make_async_remote_copy(
@@ -240,8 +241,8 @@
             mid[a, rows] = (wide(part[a, 1, rows]) + wide(land[a, 0, rows])).astype(BF16)
             yc[a][2 + half] = to(x_mate, (ys, yr), a, 2 + half, mid.at[a, rows], land.at[a, 2, rows])
 
-    def total(a):
-        for half in range(2):
+    def total(a, halves=(0, 1)):
+        for half in halves:
             rows = pl.ds(half * HALF, HALF)
             if half == 0:
                 yc[a][1].wait_recv()
@@ -263,9 +264,10 @@
     ins[...] = jnp.sum(ot[0] * wide(gt[...]), axis=0, keepdims=True)
     second(3)
     to_core(1, 0, 3)
+    total(0, (0,))
     second(1)
     to_chip(1)
-    total(0)
+    total(0, (1,))
     second(2)
     to_core(1, 1, 2)
     second(0)
@@ -314,8 +316,8 @@
             pltpu.VMEM((2, COL, D), BF16),
             pltpu.VMEM((COL, D), BF16),
             pltpu.VMEM((COL, D), BF16),
-            dma((8, 8)),
-            dma((8, 8)),
+            dma((8, 2)),
+            dma((8, 2)),
             dma((2, 3)),
             dma((2, 3)),
             dma((2, 4)),
@@ -329,17 +331,31 @@
 
 
 def handed_on_kernel(*refs):
+    given, taken, (held, come, gone) = refs[:4], refs[4:8], refs[8:]
+    into = [pltpu.make_async_copy(given[n], held.at[n], come.at[n]) for n in range(4)]
+    out = [pltpu.make_async_copy(held.at[n], taken[n], gone.at[n]) for n in range(4)]
+    for copy in into:
+        copy.start()
     for n in range(4):
-        refs[4 + n][...] = refs[n][...]
+        into[n].wait()
+        out[n].start()
+    for copy in out:
+        copy.wait()
 
 
 def handed_on(*arrays):
-    vm = pl.BlockSpec(memory_space=pltpu.VMEM)
+    anyspace = pl.BlockSpec(memory_space=pl.ANY)
     return pl.pallas_call(
         handed_on_kernel,
         out_shape=tuple(jax.ShapeDtypeStruct(a.shape, a.dtype) for a in arrays),
-        in_specs=[vm] * 4,
-        out_specs=[vm] * 4,
+        in_specs=[anyspace] * 4,
+        out_specs=[anyspace] * 4,
+        scratch_shapes=[
+            pltpu.VMEM((4,) + arrays[0].shape, arrays[0].dtype),
+            pltpu.SemaphoreType.DMA((4,)),
+            pltpu.SemaphoreType.DMA((4,)),
+        ],
+        compiler_params=pltpu.CompilerParams(vmem_limit_bytes=58 * 1024 * 1024),
         name="handed_on",
     )(*arrays)
 

time: 72.4 us -> 69.9 us (0.965)
  Pallas kernels: 71.6 us -> 69 us
    pallas_call x1, Pallas kernels: 69.5 us -> 67 us  [fused(): pl.pallas_call(fused_kernel, out_shape=(out,) * 4, in_specs=[pl.BlockSpec...]
where the time goes in v4:
time: 69.9 us; the launch traced here: 69.8 us
  Pallas kernels  69 us (99%)
  between operations  0.8 us (1%)
    pallas_call x1, Pallas kernels, fused(): pl.pallas_call(fused_kernel, out_shape=(out,) * 4, in_specs=[pl.BlockSpec...  67 us
    pallas_call x1, Pallas kernels, handed_on(): pl.pallas_call(handed_on_kernel, out_shape=tuple((jax.ShapeDtypeStruct(a....  1.98 us

profile of v4, /device:TPU:1, one launch (start us, length us, event | category | flops | bytes accessed | tf_op | source)
XLA Modules:
  0.0 69.8 jit_solution(4905880401948925344)
XLA Ops:
  0.6 67.0 %fused.1 = (bf16[128,1024]{1,0:T(8,128)(2,1)}, bf16[128,1024]{1,0:T(8,128)(2,1)}, bf16[128,1024]{1,0:T(8,128)(2,1)}, bf16[128,1024]{1,0:T(8,128)(2,1)}) custom-call(s32[12]{0:T(128)} %starts.1, bf16[128,1024]{1,0:T(8,128)(2,1)} %q_ref.1, bf16[128,1024]{1,0:T(8,128)(2,1)} %k_ref.1, bf16[128,1024]{1,0:T(8,128)(2,1)} %v_ref.1, bf16[128,1024]{1,0:T(8,128)(2,1)} %g_ref.1), custom_call_target="tpu_custom_call" | custom-call | tf_op jit(solution)/shard_map/fused/pallas_call | solution.py:290
  67.7 2.0 %handed_on.1 = (bf16[128,1024]{1,0:T(8,128)(2,1)}, bf16[128,1024]{1,0:T(8,128)(2,1)}, bf16[128,1024]{1,0:T(8,128)(2,1)}, bf16[128,1024]{1,0:T(8,128)(2,1)}) custom-call(bf16[128,1024]{1,0:T(8,128)(2,1)} %get-tuple-element.8.refs_0_, bf16[128,1024]{1,0:T(8,128)(2,1)} %get-tuple-element.9.refs_1_, bf16[128,1024]{1,0:T(8,128)(2,1)} %get-tuple-element.10.refs_2_, ...), custom_call_target="tpu_custom_call" | custom-call | tf_op jit(solution)/shard_map/handed_on/pallas_call | solution.py:348

commit v5 on v4

--- a/solution.py
+++ b/solution.py
@@ -214,7 +214,7 @@
     o = ot[0] * shares[0] + ot[1] * shares[1] + ot[2] * shares[2] + ot[3] * shares[3]
     ot[0] = o
     ob[...] = o.astype(BF16).T
-    z_start(O)
+    z_start(O, FAR)
     for j in range(NX):
         shr[j] = shares[j]
     z_arrive(G)
@@ -258,6 +258,7 @@
     to_core(0, 0, 3)
     value_part(1)
     to_chip(0)
+    z_start(O, NEAR)
     value_part(2)
     to_core(0, 1, 2)
     value_part(0)
@@ -277,10 +278,10 @@
     for copies in xc + yc:
         for copy in copies:
             copy.wait_send()
-    for a in range(4, 8):
-        z_arrive(a)
     for a in range(8):
         z_sent(a)
+        if a >= 4:
+            z_arrive(a)
 
 
 def fused(starts, q, k, v, g):

time: 69.9 us -> 69.7 us (level)
  no operation moved by 1% of the time
where the time goes in v5:
time: 69.7 us; the launch traced here: 69.6 us
  Pallas kernels  68.8 us (99%)
  between operations  0.8 us (1%)
    pallas_call x1, Pallas kernels, fused(): pl.pallas_call(fused_kernel, out_shape=(out,) * 4, in_specs=[pl.BlockSpec...  66.8 us
    pallas_call x1, Pallas kernels, handed_on(): pl.pallas_call(handed_on_kernel, out_shape=tuple((jax.ShapeDtypeStruct(a....  1.98 us

profile of v5, /device:TPU:1, one launch (start us, length us, event | category | flops | bytes accessed | tf_op | source)
XLA Modules:
  0.0 69.6 jit_solution(1075581694506311282)
XLA Ops:
  0.6 66.8 %fused.1 = (bf16[128,1024]{1,0:T(8,128)(2,1)}, bf16[128,1024]{1,0:T(8,128)(2,1)}, bf16[128,1024]{1,0:T(8,128)(2,1)}, bf16[128,1024]{1,0:T(8,128)(2,1)}) custom-call(s32[12]{0:T(128)} %starts.1, bf16[128,1024]{1,0:T(8,128)(2,1)} %q_ref.1, bf16[128,1024]{1,0:T(8,128)(2,1)} %k_ref.1, bf16[128,1024]{1,0:T(8,128)(2,1)} %v_ref.1, bf16[128,1024]{1,0:T(8,128)(2,1)} %g_ref.1), custom_call_target="tpu_custom_call" | custom-call | tf_op jit(solution)/shard_map/fused/pallas_call | solution.py:291
  67.5 2.0 %handed_on.1 = (bf16[128,1024]{1,0:T(8,128)(2,1)}, bf16[128,1024]{1,0:T(8,128)(2,1)}, bf16[128,1024]{1,0:T(8,128)(2,1)}, bf16[128,1024]{1,0:T(8,128)(2,1)}) custom-call(bf16[128,1024]{1,0:T(8,128)(2,1)} %get-tuple-element.8.refs_0_, bf16[128,1024]{1,0:T(8,128)(2,1)} %get-tuple-element.9.refs_1_, bf16[128,1024]{1,0:T(8,128)(2,1)} %get-tuple-element.10.refs_2_, ...), custom_call_target="tpu_custom_call" | custom-call | tf_op jit(solution)/shard_map/handed_on/pallas_call | solution.py:349
